TPU v7x, 256 devices: a whole 4x4x8 slice. The times are simulated.
256 devices in a mesh: row: 8 (over z_lo, y), col: 32 (over z_hi, x, core).
Axes of the slice: x: 4, y: 4, z: 8 (z_hi: 4, z_lo: 2; z = z_hi * 2 + z_lo), core: 2. Of those that a mesh axis runs over, the one named last changes fastest.
Arguments:
- matrix: float32 [8, 8, 256, 2, 32, 256], P(None, 'row', None, None, 'col'), as said below
Outputs:
- factored: float32 [8, 8, 256, 2, 32, 256], P(None, 'row', None, None, 'col')
Inputs may be any that keep to these rules, and one draw needn't show every extreme that they name: `matrix`: symmetric positive definite.
All inputs are finite; a program needn't handle non-finite values.
Results may differ from a plain program's by a relative error of at most 0.00017.
Values sent between devices are 32-bit elements; how exact they have to be, the bound alone decides.
A program may use at most 64 MiB of HBM per device.

v0:
```python
import jax
import jax.numpy as jnp
from jax import lax
from jax.sharding import PartitionSpec as P


def from_root(shard, axis, root):
    mine = lax.axis_index(axis) == root
    return lax.psum(jnp.where(mine, shard, jnp.zeros_like(shard)), axis)


def lower_solve(factor, column):
    flat_rows = column.reshape(column.shape[0] * column.shape[1], column.shape[2])
    solved = jax.scipy.linalg.solve_triangular(factor, flat_rows.T, lower=True)
    return solved.T.reshape(column.shape)


def pick_slots(pieces, grid_rows, grid_cols, col_index):
    stride = grid_cols // grid_rows
    grouped = pieces.reshape(pieces.shape[0] // stride, stride, pieces.shape[1], pieces.shape[2])
    return lax.dynamic_index_in_dim(grouped, col_index // grid_rows, 1, keepdims=False)


def diagonal_payload(corner):
    return (corner, corner)


def panel_from_diagonal(received, column):
    factor = jnp.linalg.cholesky(received)
    return (factor, lower_solve(factor, column))


def factor_panel(blocks, step_index, grid_rows, grid_cols):
    root_row = step_index % grid_rows
    slot_row = step_index // grid_rows
    slot_col = step_index // grid_cols
    own_factor, payload = diagonal_payload(blocks[slot_row, :, slot_col, :])
    received = from_root(payload, "row", root_row)
    return panel_from_diagonal(received, blocks[:, :, slot_col, :])


def apply_update(blocks, left_pieces, right_pieces):
    return blocks - jnp.einsum(
        "rin,cjn->ricj",
        left_pieces,
        right_pieces,
        precision=lax.Precision.HIGHEST,
        preferred_element_type=jnp.float32,
    )


def trailing_update(blocks, used_rows, step_index, grid_rows, grid_cols, col_index):
    left_pieces = from_root(used_rows, "col", step_index % grid_cols)
    chosen = pick_slots(left_pieces, grid_rows, grid_cols, col_index)
    right_pieces = from_root(chosen, "row", col_index % grid_rows)
    return apply_update(blocks, left_pieces, right_pieces)


def write_column(result, step_index, factor, panel_rows, global_rows, grid_cols, col_index):
    slot_col = step_index // grid_cols
    below_mask = (global_rows > step_index)[:, None, None]
    diagonal_mask = (global_rows == step_index)[:, None, None]
    column = jnp.where(below_mask, panel_rows, jnp.where(diagonal_mask, factor[None], 0.0))
    current = result[:, :, slot_col, :]
    return result.at[:, :, slot_col, :].set(
        jnp.where(col_index == step_index % grid_cols, column, current)
    )


def body(matrix):
    row_slots = matrix.shape[0]
    panel_width = matrix.shape[2]
    col_slots = matrix.shape[3]
    grid_rows = lax.axis_size("row")
    grid_cols = lax.axis_size("col")
    row_index = lax.axis_index("row")
    col_index = lax.axis_index("col")
    blocks = matrix.reshape(row_slots, panel_width, col_slots, panel_width)
    global_rows = jnp.arange(row_slots, dtype=jnp.int32) * grid_rows + row_index
    global_cols = jnp.arange(col_slots, dtype=jnp.int32) * grid_cols + col_index
    factor_first, panel_first = factor_panel(blocks, 0, grid_rows, grid_cols)
    used_first = jnp.where((global_rows > 0)[:, None, None], panel_first, 0.0)
    blocks = trailing_update(blocks, used_first, 0, grid_rows, grid_cols, col_index)
    factor_second, panel_second = factor_panel(blocks, 1, grid_rows, grid_cols)
    used_second = jnp.where((global_rows > 1)[:, None, None], panel_second, 0.0)
    blocks = trailing_update(blocks, used_second, 1, grid_rows, grid_cols, col_index)
    result = write_column(blocks, 0, factor_first, panel_first, global_rows, grid_cols, col_index)
    result = write_column(result, 1, factor_second, panel_second, global_rows, grid_cols, col_index)
    upper_mask = (global_rows[:, None] <= 1) & (global_cols[None, :] > global_rows[:, None])
    result = jnp.where(upper_mask[:, None, :, None], 0.0, result)
    return result.reshape(matrix.shape)


def solution(mesh):
    in_specs = (P(None, "row", None, None, "col", None),)
    out_specs = P(None, "row", None, None, "col", None)
    return jax.shard_map(body, mesh=mesh, in_specs=in_specs, out_specs=out_specs, check_vma=False)
```

profile of v0, /device:TPU:117, one launch (start us, length us, event | category | flops | bytes accessed | tf_op | source)
XLA Modules:
  0.0 1098.8 jit_solution(17983322274684691133)
XLA Ops:
  6.5 10.9 copy.31
  21.0 1.9 copy.33
  22.9 1.9 copy.34
  24.8 68.6 %all-reduce.8.cloned.1.call-done = f32[256,256]{0,1:T(8,128)} async-done(((f32[256,256]{0,1:T(8,128)}), f32[256,256]{0,1:T(8,128)}) %all-reduce.8.cloned.1.call-update) | async-done | bytes 262160 | tf_op jit(solution)/shard_map/psum | solution.py:9
  95.5 11.7 %cholesky.130 = f32[128,128]{1,0:T(8,128)S(1)} custom-call(f32[128,128]{1,0:T(8,128)S(1)} %cholesky.194), custom_call_target="Cholesky" | custom-call | tf_op jit(solution)/shard_map/jit(cholesky)/cholesky | solution.py:29
  107.2 9.8 custom-call.13
  117.6 11.7 %cholesky.147 = f32[128,128]{1,0:T(8,128)S(1)} custom-call(f32[128,128]{1,0:T(8,128)S(1)} %convolution_subtract_fusion.5), custom_call_target="Cholesky" | custom-call | tf_op jit(solution)/shard_map/jit(cholesky)/cholesky | solution.py:29
  131.4 4.1 while.6
  135.5 20.2 %custom-call.14 = f32[2,128,128]{1,2,0:T(8,128)S(1)} custom-call(f32[2,128,128]{2,1,0:T(8,128)S(1)} %get-tuple-element.45), custom_call_target="InvertDiagBlocksLowerTriangular" | custom-call | tf_op jit(solution)/shard_map/jit(_solve_triangular)/triangular_solve | solution.py:14
  160.3 1.9 copy.55
  164.3 293.4 %all-reduce.10.cloned.1.call-done = f32[8,256,256]{2,1,0:T(8,128)} async-done(((f32[8,256,256]{2,1,0:T(8,128)}), f32[8,256,256]{2,1,0:T(8,128)}) %all-reduce.10.cloned.1.call-update) | async-done | bytes 2097168 | tf_op jit(solution)/shard_map/psum | solution.py:9
  457.7 1.9 fusion.7
  459.7 77.1 %all-reduce.12.cloned.1.call-done = f32[2,256,256]{2,1,0:T(8,128)} async-done(((f32[2,256,256]{2,1,0:T(8,128)}), f32[2,256,256]{2,1,0:T(8,128)}) %all-reduce.12.cloned.1.call-update) | async-done | bytes 524304 | tf_op jit(solution)/shard_map/psum | solution.py:9
  536.8 7.0 convolution_subtract_fusion.3
  543.8 2.0 copy-done
  548.2 2.0 copy.39
  550.2 1.9 copy.40
  552.1 73.3 %all-reduce.14.cloned.1.call-done = f32[256,256]{0,1:T(8,128)} async-done(((f32[256,256]{0,1:T(8,128)}), f32[256,256]{0,1:T(8,128)}) %all-reduce.14.cloned.1.call-update) | async-done | bytes 262160 | tf_op jit(solution)/shard_map/psum | solution.py:9
  627.5 11.7 %cholesky.164 = f32[128,128]{1,0:T(8,128)S(1)} custom-call(f32[128,128]{1,0:T(8,128)S(1)} %cholesky.197), custom_call_target="Cholesky" | custom-call | tf_op jit(solution)/shard_map/jit(cholesky)/cholesky | solution.py:29
  639.9 9.8 custom-call.15
  650.2 11.7 %cholesky.181 = f32[128,128]{1,0:T(8,128)S(1)} custom-call(f32[128,128]{1,0:T(8,128)S(1)} %convolution_subtract_fusion.4), custom_call_target="Cholesky" | custom-call | tf_op jit(solution)/shard_map/jit(cholesky)/cholesky | solution.py:29
  663.9 3.9 while.7
  667.8 19.9 %custom-call.16 = f32[2,128,128]{1,2,0:T(8,128)S(1)} custom-call(f32[2,128,128]{2,1,0:T(8,128)S(1)} %get-tuple-element.46), custom_call_target="InvertDiagBlocksLowerTriangular" | custom-call | tf_op jit(solution)/shard_map/jit(_solve_triangular)/triangular_solve | solution.py:14
  692.3 1.9 copy.41
  696.3 293.5 %all-reduce.16.cloned.1.call-done = f32[8,256,256]{2,1,0:T(8,128)} async-done(((f32[8,256,256]{2,1,0:T(8,128)}), f32[8,256,256]{2,1,0:T(8,128)}) %all-reduce.16.cloned.1.call-update) | async-done | bytes 2097168 | tf_op jit(solution)/shard_map/psum | solution.py:9
  989.7 1.9 fusion.6
  992.0 2.1 copy.46
  994.3 1.9 copy.49
  996.2 72.7 %all-reduce.18.cloned.1.call-done = f32[2,256,256]{2,1,0:T(8,128)} async-done(((f32[2,256,256]{2,1,0:T(8,128)}), f32[2,256,256]{2,1,0:T(8,128)}) %all-reduce.18.cloned.1.call-update) | async-done | bytes 524304 | tf_op jit(solution)/shard_map/psum | solution.py:9
  1068.9 6.5 convolution_subtract_fusion.2
  1078.4 2.4 select_bitcast_fusion
  1080.8 10.9 copy.50
  (86 shorter events, 37.9 us)
Async XLA Ops:
  6.5 86.9 %all-reduce.8.cloned.1.call-start = ((), (), s32[]{:S(2)}) async-start(), calls=%async_computation | async-start | bytes 524288 | tf_op jit(solution)/shard_map/psum | solution.py:9
  19.1 438.6 %all-reduce.10.cloned.1.call-start = ((), (), s32[]{:S(2)}) async-start(), calls=%async_computation.1 | async-start | bytes 4194304 | tf_op jit(solution)/shard_map/psum | solution.py:9
  162.3 1.9 copy-start.1
  164.2 372.6 %all-reduce.12.cloned.1.call-start = ((), (), s32[]{:S(2)}) async-start(), calls=%async_computation.2 | async-start | bytes 1048576 | tf_op jit(solution)/shard_map/psum | solution.py:9
  459.6 165.8 %all-reduce.14.cloned.1.call-start = ((), (), s32[]{:S(2)}) async-start(), calls=%async_computation.3 | async-start | bytes 524288 | tf_op jit(solution)/shard_map/psum | solution.py:9
  543.8 2.0 copy-start
  546.6 443.2 %all-reduce.16.cloned.1.call-start = ((), (), s32[]{:S(2)}) async-start(), calls=%async_computation.4 | async-start | bytes 4194304 | tf_op jit(solution)/shard_map/psum | solution.py:9
  546.6 1.6 slice-start
  694.2 2.0 copy-start.3
  696.2 295.8 %copy-start.2 = (f32[2048,256]{1,0:T(8,128)S(1)}, f32[2048,256]{1,0:T(8,128)}, u32[]{:S(2)}) copy-start(f32[2048,256]{1,0:T(8,128)} %copy-done.1) | copy-start | bytes 6291460
  696.2 372.7 %all-reduce.18.cloned.1.call-start = ((), (), s32[]{:S(2)}) async-start(), calls=%async_computation.5 | async-start | bytes 1048576 | tf_op jit(solution)/shard_map/psum | solution.py:9
  1075.4 1.6 copy-start.4
Sparse Core Ops, SparseCore 0:
  19.2 74.1 all-reduce.7
  164.4 293.3 all-reduce.9
  460.4 76.3 all-reduce.11
  546.7 78.6 all-reduce.13
  696.3 293.3 all-reduce.15
  992.4 76.4 all-reduce.17
where the time goes:
time: 1120 us; the launch traced here: 1100 us
  waiting for transfers between devices  879 us (78%)
  other arithmetic  128 us (11%)
  local copies, waits for them, and re-layouts  55 us (5%)
  matrix products  20.7 us (2%)
  between operations  16.7 us (1%)
    psum x6, waiting for transfers between devices, from_root(): return lax.psum(jnp.where(mine, shard, jnp.zeros_like(shard)), axis)  879 us
    another operation x13, other arithmetic, panel_from_diagonal(): factor = jnp.linalg.cholesky(received)  68.7 us
    another operation x5, other arithmetic, lower_solve(): solved = jax.scipy.linalg.solve_triangular(factor, flat_rows.T, lower=True)  40.2 us
  transfers between devices with their start and end apart: 6, of which 6 were waited for; matrix products, arithmetic and copies ran while one was open for 1% of the time, Pallas kernels for 0%

commit v1 on v0

v1 whole, which is shorter than its diff:
```python
import functools

import jax
import jax.numpy as jnp
from jax import lax
from jax.experimental import pallas as pl
from jax.experimental.pallas import tpu as pltpu
from jax.sharding import PartitionSpec as P

F32 = jnp.float32
BF16 = jnp.bfloat16
MESH = pl.DeviceIdType.MESH
HIGHEST = lax.Precision.HIGHEST
NB = 256
LEAF = 128
CHUNKS = [(i, j) for i in range(4) for j in range(i + 1)]


def leaf_inverse(block):
    n = block.shape[0]
    sub = lax.broadcasted_iota(jnp.int32, (8, n), 0)
    lane = lax.broadcasted_iota(jnp.int32, (8, n), 1)
    rows = [block[8 * g : 8 * g + 8] for g in range(n // 8)]
    inv = [jnp.where(lane == sub + 8 * g, 1.0, 0.0).astype(F32) for g in range(n // 8)]
    out = []
    for t in range(n // 8):
        cols = [[jnp.broadcast_to(r[:, 8 * t + j : 8 * t + j + 1], (8, n)) for r in rows] for j in range(8)]
        for j in range(8):
            r = lax.rsqrt(jnp.broadcast_to(cols[j][0][j : j + 1], (8, n)))
            lcol = [c * r for c in cols[j]]
            lead = lcol[0]
            for k in range(j + 1, 8):
                f = jnp.broadcast_to(lead[k : k + 1], (8, n))
                cols[k] = [c - l * f for c, l in zip(cols[k], lcol)]
            row = jnp.broadcast_to(rows[0][j : j + 1], (8, n)) * r
            irow = jnp.broadcast_to(inv[0][j : j + 1], (8, n)) * r
            low = jnp.where(sub > j, lead, 0.0)
            rows = [rows[0] - low * row] + [a - l * row for a, l in zip(rows[1:], lcol[1:])]
            inv = [jnp.where(sub == j, irow, inv[0] - low * irow)] + [a - l * irow for a, l in zip(inv[1:], lcol[1:])]
        out.append(inv[0])
        rows, inv = rows[1:], inv[1:]
    return jnp.concatenate(out, 0)


def dot_full(a, b, trans_a=False):
    return lax.dot_general(
        a, b, (((0 if trans_a else 1,), (0,)), ((), ())), precision=HIGHEST, preferred_element_type=F32
    )


def factor_block(i, nb, d_ref, li_ref):
    n = LEAF
    s = slice(i * n, (i + 1) * n)
    m = leaf_inverse(d_ref[s, s])
    li_ref[s, s] = m
    if i:
        li_ref[s, : i * n] = -dot_full(m, d_ref[s, : i * n])
    if i + 1 < nb:
        r = dot_full(m, d_ref[s, (i + 1) * n :])
        for j in range(i + 1, nb):
            off = (j - i - 1) * n
            t = slice(j * n, (j + 1) * n)
            rj = r[:, off : off + n]
            d_ref[t, j * n :] = d_ref[t, j * n :] - dot_full(rj, r[:, off:], True)
            p = dot_full(rj, li_ref[s, : (i + 1) * n], True)
            if i:
                d_ref[t, : i * n] = d_ref[t, : i * n] + p[:, : i * n]
            d_ref[t, s] = p[:, i * n :]


def gather_kernel(x_ref, ar_ref, ac_ref, lo_ref, xin, xb, xt, d, li,
                  in_sem, loc_sem, sc_s, sc_r, zb_s, zb_r, xc_s, xc_r, cd_s, cd_r,
                  lc_s, lc_r, dg_s, dg_r, li_s, li_r):
    row = lax.axis_index("row")
    col = lax.axis_index("col")
    zl, y = row // 4, row % 4
    zh, x, co = col // 8, (col // 2) % 4, col % 2

    def dev(zl=zl, y=y, zh=zh, x=x, co=co):
        return (zl * 4 + y, (zh * 4 + x) * 2 + co)

    def rc(src, dst, ss, rs, to):
        return pltpu.make_async_remote_copy(
            src_ref=src, dst_ref=dst, send_sem=ss, recv_sem=rs, device_id=to, device_id_type=MESH
        )

    def piece(p, xq, zq):
        at = pl.multiple_of((4 * (xq // 2) + zq) * NB + (xq % 2) * LEAF, LEAF)
        return ar_ref.at[p, pl.ds(at, LEAF), :]

    top = row < 2
    root = (row == 0) & (col == 0)
    self_scatter = (row == co) & (x == 0)
    here = dev()

    is_z = (row == 0) & (col == 0)
    is_x = (row == 0) & (x == 0) & (co == 0)
    is_y = (row == 0) & (co == 0)
    is_l = (zl == 0) & (co == 0)
    is_c = co == 0

    load = pltpu.make_async_copy(x_ref.at[pl.ds(0, 4 * NB)], xin, in_sem)

    @pl.when(top)
    def _():
        load.start()

    bar = pltpu.get_barrier_semaphore()

    def greet(to):
        pl.semaphore_signal(bar, inc=1, device_id=to, device_id_type=MESH)

    one = lambda c: jnp.where(c, 1, 0)

    @pl.when(jnp.logical_not(self_scatter))
    def _():
        greet((co, zh * 8 + row))

    for k in range(1, 4):
        greet(dev(zh=(zh + k) % 4))
        greet(dev(x=(x + k) % 4))
    greet(dev(co=1 - co))
    edges = 7 + jnp.where(top, 4 - one(col % 8 == row), 0)
    for p in range(2):
        near, far, mid = (1, 2, 3) if p == 0 else (0, 3, 2)

        @pl.when((row == p + 4))
        def _():
            greet(dev(zl=0))

        @pl.when((y == near) | (y == mid))
        def _():
            greet(dev(y=p))

        @pl.when(y == far)
        def _():
            greet(dev(y=mid))

        edges = edges + 2 * one(y == p) + one(row == p) + one(y == mid)

    @pl.when(root)
    def _():
        greet((0, 1))
        greet((1, 1))

    edges = edges + one((row < 2) & (col == 1))

    @pl.when(jnp.logical_not(is_c))
    def _():
        greet(dev(co=0))

    @pl.when(is_c & jnp.logical_not(is_l))
    def _():
        greet(dev(zl=0))

    @pl.when(is_l & jnp.logical_not(is_y))
    def _():
        greet(dev(y=0))

    @pl.when(is_y & jnp.logical_not(is_x))
    def _():
        greet(dev(x=0))

    @pl.when(is_x & jnp.logical_not(is_z))
    def _():
        greet(dev(zh=0))

    edges = edges + 3 * one(is_z) + 3 * one(is_x) + 3 * one(is_y) + one(is_l) + one(is_c)
    pl.semaphore_wait(bar, edges)


    def scatter(q):
        return rc(xt.at[pl.ds(q * LEAF, LEAF)],
                  ar_ref.at[row, pl.ds(pl.multiple_of((4 * (q // 2) + zh) * NB + (q % 2) * LEAF, LEAF), LEAF), :],
                  sc_s.at[q], sc_r.at[0], (col % 8, (zh * 4 + q) * 2 + row))

    def scatter_in():
        return rc(piece(co, x, zh), piece(co, x, zh), sc_s.at[0], sc_r.at[0], dev(co=1 - co))

    def scatter_self():
        return pltpu.make_async_copy(xt.at[pl.ds(0, LEAF)], piece(co, x, zh), loc_sem.at[0])

    def z_out(k):
        return rc(piece(co, x, zh), piece(co, x, zh), zb_s.at[k - 1], zb_r.at[k - 1], dev(zh=(zh + k) % 4))

    def z_in(k):
        q = piece(co, x, (zh + 4 - k) % 4)
        return rc(q, q, zb_s.at[k - 1], zb_r.at[k - 1], dev(co=1 - co))

    def x_out(kz, kx):
        q = piece(co, x, (zh + 4 - kz) % 4)
        return rc(q, q, xc_s.at[kz, kx - 1], xc_r.at[kz, kx - 1], dev(x=(x + kx) % 4))

    def x_in(kz, kx):
        q = piece(co, (x + 4 - kx) % 4, (zh + 4 - kz) % 4)
        return rc(q, q, xc_s.at[kz, kx - 1], xc_r.at[kz, kx - 1], dev(co=1 - co))

    def c_out(kz, kx):
        q = piece(co, (x + 4 - kx) % 4, (zh + 4 - kz) % 4)
        return rc(q, q, cd_s.at[kz, kx], cd_r.at[kz, kx], dev(co=1 - co))

    def c_in(kz, kx):
        q = piece(1 - co, (x + 4 - kx) % 4, (zh + 4 - kz) % 4)
        return rc(q, q, cd_s.at[kz, kx], cd_r.at[kz, kx], dev(co=1 - co))

    def lc_part(p, h):
        return ac_ref.at[pl.ds(p * NB + h * LEAF, LEAF)]

    def lc_first(p, h, k):
        to = (dev(zl=1), dev(y=(p + 1) % 4), dev(y=(p + 3) % 4))[k]
        return rc(xb.at[pl.ds(h * LEAF, LEAF)], lc_part(p, h), lc_s.at[p, h, k], lc_r.at[p, h], to)

    def lc_next(p, h, k, to):
        return rc(lc_part(p, h), lc_part(p, h), lc_s.at[p, h, k], lc_r.at[p, h], to)

    def lc_in(p, h):
        return rc(lc_part(p, h), lc_part(p, h), lc_s.at[p, h, 0], lc_r.at[p, h], dev(co=1 - co))

    def diag_out(p):
        return rc(xb.at[:, pl.ds(0, NB)], d.at[pl.ds(p * NB, NB), pl.ds(NB, NB)], dg_s.at[0], dg_r.at[p], (0, 0))

    def diag_in(p):
        q = d.at[pl.ds(p * NB, NB), pl.ds(NB, NB)]
        return rc(q, q, dg_s.at[0], dg_r.at[p], (0, 1))

    def li_part(ref, c):
        i, j = CHUNKS[c]
        return ref.at[pl.ds(i * LEAF, LEAF), pl.ds(j * LEAF, LEAF)]

    def li_out(c, ref, k, to):
        return rc(li_part(ref, c), li_part(lo_ref, c), li_s.at[c, k], li_r.at[c], to)

    def li_in(c):
        q = li_part(lo_ref, c)
        return rc(q, q, li_s.at[c, 0], li_r.at[c], dev(co=1 - co))

    def li_edges(c, ref, what):
        def run(role, k, to):
            @pl.when(role)
            def _():
                cp = li_out(c, ref, k, to)
                cp.start() if what == "start" else cp.wait_send()

        for k in range(3):
            run(is_z, k, dev(zh=(zh + k + 1) % 4))
        for k in range(3):
            run(is_x, 3 + k, dev(x=(x + k + 1) % 4))
        for k in range(3):
            run(is_y, 6 + k, dev(y=(y + k + 1) % 4))
        run(is_l, 9, dev(zl=1))
        run(is_c, 10, dev(co=1))

    def li_pass(chunks):
        @pl.when(jnp.logical_not(root))
        def _():
            for c in chunks:
                li_in(c).wait_recv()
                li_edges(c, lo_ref, "start")

    def li_root(i):
        @pl.when(root)
        def _():
            if i == 0:
                d[pl.ds(0, NB), pl.ds(0, NB)] = xb[:, pl.ds(0, NB)]
                for p in range(2):
                    diag_in(p).wait_recv()
            factor_block(i, 4, d, li)
            for c, (a, _b) in enumerate(CHUNKS):
                if a == i:
                    li_edges(c, li, "start")
                    pltpu.make_async_copy(li_part(li, c), li_part(lo_ref, c), loc_sem.at[4 + c]).start()


    for p in range(2):

        @pl.when(row == p)
        def _():
            load.wait()
            for q in range(4):
                xb[:, pl.ds(q * LEAF, LEAF)] = xin[pl.ds(q, NB, stride=4), :]

            @pl.when(col == 1)
            def _():
                diag_out(p).start()

            for k in range(3):
                lc_first(p, 0, k).start()
            for q in range(4):
                xt[pl.ds(q * LEAF, LEAF), :] = xb[:, pl.ds(q * LEAF, LEAF)].T
            for q in range(1, 4):
                scatter(q).start()

            @pl.when(col % 8 == row)
            def _():
                scatter_self().start()

            @pl.when(col % 8 != row)
            def _():
                scatter(0).start()

            for k in range(3):
                lc_first(p, 1, k).start()
            pltpu.make_async_copy(xb, ac_ref.at[pl.ds(p * NB, NB)], loc_sem.at[1]).start()

    li_root(0)


    @pl.when(self_scatter)
    def _():
        scatter_self().wait()

    @pl.when(jnp.logical_not(self_scatter))
    def _():
        scatter_in().wait_recv()

    for k in range(1, 4):
        z_out(k).start()
        x_out(0, k).start()
    c_out(0, 0).start()

    li_root(1)

    for h in range(2):
        for p in range(2):
            near, far, mid = (1, 2, 3) if p == 0 else (0, 3, 2)

            @pl.when(row == p + 4)
            def _():
                lc_in(p, h).wait_recv()
                lc_next(p, h, 1, dev(y=(p + 1) % 4)).start()
                lc_next(p, h, 2, dev(y=(p + 3) % 4)).start()

            @pl.when(y == mid)
            def _():
                lc_in(p, h).wait_recv()
                lc_next(p, h, 0, dev(y=far)).start()

    li_root(2)

    for kz in range(1, 4):
        z_in(kz).wait_recv()
        for kx in range(1, 4):
            x_out(kz, kx).start()
        c_out(kz, 0).start()

    li_root(3)

    parts = [[0, 1, 2], [3, 4, 5], [], [6, 7, 8, 9]]
    for kz in range(4):
        for kx in range(1, 4):
            x_in(kz, kx).wait_recv()
            c_out(kz, kx).start()
        li_pass(parts[kz])

    for h in range(2):
        for p in range(2):
            near, far, mid = (1, 2, 3) if p == 0 else (0, 3, 2)

            @pl.when((y == near) | (y == far))
            def _():
                lc_in(p, h).wait_recv()

    for kz in range(4):
        for kx in range(4):
            c_in(kz, kx).wait_recv()
            c_out(kz, kx).wait_send()
            if kx:
                x_out(kz, kx).wait_send()
        if kz:
            z_out(kz).wait_send()

    for p in range(2):

        @pl.when(row == p)
        def _():
            @pl.when(col == 1)
            def _():
                diag_out(p).wait_send()

            for h in range(2):
                for k in range(3):
                    lc_first(p, h, k).wait_send()
            for q in range(1, 4):
                scatter(q).wait_send()

            @pl.when(col % 8 != row)
            def _():
                scatter(0).wait_send()

            pltpu.make_async_copy(xb, ac_ref.at[pl.ds(p * NB, NB)], loc_sem.at[1]).wait()

        near, far, mid = (1, 2, 3) if p == 0 else (0, 3, 2)
        for h in range(2):

            @pl.when(row == p + 4)
            def _():
                lc_next(p, h, 1, dev(y=(p + 1) % 4)).wait_send()
                lc_next(p, h, 2, dev(y=(p + 3) % 4)).wait_send()

            @pl.when(y == mid)
            def _():
                lc_next(p, h, 0, dev(y=far)).wait_send()

    for c in range(len(CHUNKS)):
        li_edges(c, lo_ref, "wait")

        @pl.when(root)
        def _():
            pltpu.make_async_copy(li_part(li, c), li_part(lo_ref, c), loc_sem.at[4 + c]).wait()


def gather(flat):
    any_spec = pl.BlockSpec(memory_space=pl.ANY)
    dma = pltpu.SemaphoreType.DMA
    return pl.pallas_call(
        gather_kernel,
        out_shape=[
            jax.ShapeDtypeStruct((2, 2048, NB), F32),
            jax.ShapeDtypeStruct((2 * NB, 2 * NB), F32),
            jax.ShapeDtypeStruct((2 * NB, 2 * NB), F32),
        ],
        in_specs=[any_spec],
        out_specs=[any_spec] * 3,
        scratch_shapes=[
            pltpu.VMEM((4 * NB, 128), F32),
            pltpu.VMEM((NB, 2 * NB), F32),
            pltpu.VMEM((2 * NB, NB), F32),
            pltpu.VMEM((2 * NB, 2 * NB), F32),
            pltpu.VMEM((2 * NB, 2 * NB), F32),
            dma, dma((14,)),
            dma((4,)), dma((1,)),
            dma((3,)), dma((3,)),
            dma((4, 3)), dma((4, 3)),
            dma((4, 4)), dma((4, 4)),
            dma((2, 2, 3)), dma((2, 2)),
            dma((1,)), dma((2,)),
            dma((10, 11)), dma((10,)),
        ],
        compiler_params=pltpu.CompilerParams(collective_id=0, has_side_effects=True, vmem_limit_bytes=32 << 20),
        name="gather_panel",
    )(flat)


def halves(a):
    hi = a.astype(BF16)
    return hi, (a - hi.astype(F32)).astype(BF16)


def dot3(a, b, trans_b=False):
    dims = (((1,), (1 if trans_b else 0,)), ((), ()))
    mm = lambda u, v: lax.dot_general(u, v, dims, preferred_element_type=F32)
    return mm(a[0], b[0]) + (mm(a[0], b[1]) + mm(a[1], b[0]))


def update_kernel(x_ref, ar_ref, ac_ref, li_ref, o_ref, u_hi, u_lo, l_hi, l_lo):
    slot = pl.program_id(0)
    row = lax.axis_index("row")
    col = lax.axis_index("col")

    @pl.when(slot == 0)
    def _():
        for i in range(4):
            for j in range(4):
                at = (pl.ds(i * LEAF, LEAF), pl.ds(j * LEAF, LEAF))
                if j > i:
                    l_hi[at] = jnp.zeros((LEAF, LEAF), BF16)
                    l_lo[at] = jnp.zeros((LEAF, LEAF), BF16)
                else:
                    v = li_ref[at]
                    if i == j:
                        r = lax.broadcasted_iota(jnp.int32, v.shape, 0)
                        c = lax.broadcasted_iota(jnp.int32, v.shape, 1)
                        v = jnp.where(c <= r, v, 0.0)
                    l_hi[at], l_lo[at] = halves(v)
        u = dot3((l_hi[...], l_lo[...]), halves(ac_ref[...]))
        u_hi[...], u_lo[...] = halves(u)

    a0 = halves(ar_ref[0])
    a1 = halves(ar_ref[1])
    top, low = pl.ds(0, NB), pl.ds(NB, NB)
    p0 = dot3(a0, (l_hi[top, top], l_lo[top, top]), True)
    p1 = dot3(a0, (l_hi[low, top], l_lo[low, top]), True) + dot3(a1, (l_hi[low, low], l_lo[low, low]), True)
    h0, h1 = halves(p0), halves(p1)
    upd = dot3(h0, (u_hi[top, :], u_lo[top, :])) + dot3(h1, (u_hi[low, :], u_lo[low, :]))
    grow = slot * 8 + row
    keep = grow >= 2
    for q in range(4):
        cols = slice(q * LEAF, (q + 1) * LEAF)
        v = jnp.where(keep, x_ref[0, pl.ds(q, NB, stride=4), :] - upd[:, cols], 0.0)
        o_ref[0, pl.ds(q, NB, stride=4), :] = v

    def put(p, mask):
        for q in range(2):
            v = p[:, q * LEAF : (q + 1) * LEAF]
            r = lax.broadcasted_iota(jnp.int32, v.shape, 0)
            c = lax.broadcasted_iota(jnp.int32, v.shape, 1) + q * LEAF
            o_ref[0, pl.ds(q, NB, stride=4), :] = jnp.where((c <= r) | jnp.logical_not(mask), v, 0.0)

    @pl.when(col == 0)
    def _():
        put(p0, grow == 0)

    @pl.when((col == 1) & (grow >= 1))
    def _():
        put(p1, grow == 1)


def update(flat, ar, ac, li):
    whole = pl.BlockSpec((2 * NB, 2 * NB), lambda s: (0, 0))
    slab = pl.BlockSpec((1, 4 * NB, 128), lambda s: (s, 0, 0))
    return pl.pallas_call(
        update_kernel,
        grid=(8,),
        out_shape=jax.ShapeDtypeStruct(flat.shape, F32),
        in_specs=[slab, pl.BlockSpec((2, NB, NB), lambda s: (0, s, 0)), whole, whole],
        out_specs=slab,
        scratch_shapes=[pltpu.VMEM((2 * NB, 2 * NB), BF16)] * 4,
        compiler_params=pltpu.CompilerParams(vmem_limit_bytes=32 << 20),
        name="update_trailing",
    )(flat, ar, ac, li)


def body(matrix):
    flat = matrix.reshape(8 * 4 * NB, 128)
    ar, ac, li = gather(flat)
    return update(flat.reshape(8, 4 * NB, 128), ar, ac, li).reshape(matrix.shape)


def solution(mesh):
    spec = P(None, "row", None, None, "col", None)
    return jax.shard_map(body, mesh=mesh, in_specs=(spec,), out_specs=spec, check_vma=False)
```

time: 1120 us -> 89.4 us (0.08); the launches traced: 1100 us -> 89.3 us
  waiting for transfers between devices: 879 us -> 0 us
  other arithmetic: 128 us -> 0 us
  Pallas kernels: 0 us -> 87.1 us
  local copies, waits for them, and re-layouts: 55 us -> 2.19 us
  matrix products: 20.7 us -> 0 us
  between operations: 16.7 us -> 0.01 us
    psum x6 -> x0, waiting for transfers between devices: 879 us -> none  [from_root(): return lax.psum(jnp.where(mine, shard, jnp.zeros_like(shard)), axis)]
    another operation x18 -> x0, other arithmetic: 109 us -> none  [the longest x13 68.7 us: panel_from_diagonal(): factor = jnp.linalg.cholesky(received)]
    pallas_call x0 -> x2, Pallas kernels: none -> 87.1 us  [the longest x1 74.5 us: gather(): pl.pallas_call(gather_kernel, out_shape=[jax.ShapeDtypeStruct((2, 2048, N...]
    reshape x4 -> x0, local copies, waits for them, and re-layouts: 16.8 us -> none  [the longest x1 10.9 us: body(): return result.reshape(matrix.shape)]
    dot_general x2 -> x0, matrix products: 13.6 us -> none  [apply_update(): jnp.einsum('rin,cjn->ricj', left_pieces, right_pieces, precision=lax.Prec...]
    unnamed x12 -> x2, local copies, waits for them, and re-layouts: 14.6 us -> 2.19 us
    another operation x21 -> x0, local copies, waits for them, and re-layouts: 11.8 us -> none  [the longest x15 7.94 us: lower_solve(): solved = jax.scipy.linalg.solve_triangular(factor, flat_rows.T, lower=True)]
  transfers between devices with their start and end apart: 6 -> 0, of which waited for: 6 -> 0; matrix products, arithmetic and copies ran while one was open for 1% -> 0% of each run, Pallas kernels for 0% -> 0%
where the time goes in v1:
time: 89.4 us; the launch traced here: 89.3 us
  Pallas kernels  87.1 us (97%)
  local copies, waits for them, and re-layouts  2.19 us (2%)
    pallas_call x1, Pallas kernels, gather(): pl.pallas_call(gather_kernel, out_shape=[jax.ShapeDtypeStruct((2, 2048, N...  74.5 us
    pallas_call x1, Pallas kernels, update(): pl.pallas_call(update_kernel, grid=(8,), out_shape=jax.ShapeDtypeStruct(f...  12.6 us
    unnamed x2, local copies, waits for them, and re-layouts  2.19 us

profile of v1, /device:TPU:117, one launch (start us, length us, event | category | flops | bytes accessed | tf_op | source)
XLA Modules:
  0.0 89.3 jit_solution(7354049744066902441)
XLA Ops:
  0.0 0.0 copy-start
  0.0 2.2 %copy-done = f32[8,1,256,2,1,256]{5,4,3,2,1,0:T(1,128)S(1)} copy-done((f32[8,1,256,2,1,256]{5,4,3,2,1,0:T(1,128)S(1)}, f32[8,1,256,2,1,256]{5,4,3,2,1,0:T(1,128)}, u32[]{:S(2)}) %copy-start) | copy-done | bytes 4194328
  2.2 74.5 %gather_panel.1 = (f32[2,2048,256]{2,1,0:T(8,128)S(1)}, f32[512,512]{1,0:T(8,128)S(1)}, f32[512,512]{1,0:T(8,128)S(1)}) custom-call(f32[8192,128]{1,0:T(8,128)S(1)} %bitcast.3), custom_call_target="tpu_custom_call" | custom-call | tf_op jit(solution)/shard_map/gather_panel/pallas_call | solution.py:415
  76.7 12.6 %update_trailing.1 = f32[8,1024,128]{2,1,0:T(8,128)} custom-call(f32[8,1024,128]{2,1,0:T(8,128)S(1)} %bitcast.4, f32[2,2048,256]{2,1,0:T(8,128)S(1)} %get-tuple-element.8.ar_ref, f32[512,512]{1,0:T(8,128)S(1)} %get-tuple-element.9.ac_ref, f32[512,512]{1,0:T(8,128)S(1)} %get-tuple-element.10.li_ref), custom_call_target="tpu_custom_call" | custom-call | tf_op jit(solution)/shard_map/update_trailing/pallas_call | solution.py:511
Async XLA Ops:
  0.0 2.2 %copy-start = (f32[8,1,256,2,1,256]{5,4,3,2,1,0:T(1,128)S(1)}, f32[8,1,256,2,1,256]{5,4,3,2,1,0:T(1,128)}, u32[]{:S(2)}) copy-start(f32[8,1,256,2,1,256]{5,4,3,2,1,0:T(1,128)} %param.1) | copy-start | bytes 12582916

commit v2 on v1

v2 whole, which is shorter than its diff:
```python
import jax
import jax.numpy as jnp
from jax import lax
from jax.experimental import pallas as pl
from jax.experimental.pallas import tpu as pltpu
from jax.sharding import PartitionSpec as P

F32 = jnp.float32
BF16 = jnp.bfloat16
MESH = pl.DeviceIdType.MESH
HIGHEST = lax.Precision.HIGHEST
NB = 256
LEAF = 128
CHUNKS = [(i, j) for i in range(4) for j in range(i + 1)]


def leaf_inverse(block):
    n = block.shape[0]
    sub = lax.broadcasted_iota(jnp.int32, (8, n), 0)
    lane = lax.broadcasted_iota(jnp.int32, (8, n), 1)
    rows = [block[8 * g : 8 * g + 8] for g in range(n // 8)]
    inv = [jnp.where(lane == sub + 8 * g, 1.0, 0.0).astype(F32) for g in range(n // 8)]
    out = []
    for t in range(n // 8):
        cols = [[jnp.broadcast_to(r[:, 8 * t + j : 8 * t + j + 1], (8, n)) for r in rows] for j in range(8)]
        for j in range(8):
            r = lax.rsqrt(jnp.broadcast_to(cols[j][0][j : j + 1], (8, n)))
            lcol = [c * r for c in cols[j]]
            lead = lcol[0]
            for k in range(j + 1, 8):
                f = jnp.broadcast_to(lead[k : k + 1], (8, n))
                cols[k] = [c - l * f for c, l in zip(cols[k], lcol)]
            row = jnp.broadcast_to(rows[0][j : j + 1], (8, n)) * r
            irow = jnp.broadcast_to(inv[0][j : j + 1], (8, n)) * r
            low = jnp.where(sub > j, lead, 0.0)
            rows = [rows[0] - low * row] + [a - l * row for a, l in zip(rows[1:], lcol[1:])]
            inv = [jnp.where(sub == j, irow, inv[0] - low * irow)] + [a - l * irow for a, l in zip(inv[1:], lcol[1:])]
        out.append(inv[0])
        rows, inv = rows[1:], inv[1:]
    return jnp.concatenate(out, 0)


def dot_full(a, b, trans_a=False):
    return lax.dot_general(
        a, b, (((0 if trans_a else 1,), (0,)), ((), ())), precision=HIGHEST, preferred_element_type=F32
    )


def factor_block(i, nb, d_ref, li_ref):
    n = LEAF
    s = slice(i * n, (i + 1) * n)
    m = leaf_inverse(d_ref[s, s])
    li_ref[s, s] = m
    if i:
        li_ref[s, : i * n] = -dot_full(m, d_ref[s, : i * n])
    if i + 1 < nb:
        r = dot_full(m, d_ref[s, (i + 1) * n :])
        for j in range(i + 1, nb):
            off = (j - i - 1) * n
            t = slice(j * n, (j + 1) * n)
            rj = r[:, off : off + n]
            d_ref[t, j * n :] = d_ref[t, j * n :] - dot_full(rj, r[:, off:], True)
            p = dot_full(rj, li_ref[s, : (i + 1) * n], True)
            if i:
                d_ref[t, : i * n] = d_ref[t, : i * n] + p[:, : i * n]
            d_ref[t, s] = p[:, i * n :]


def factor_first(d_ref, li_ref):
    n = LEAF
    m = leaf_inverse(d_ref[:n, :n])
    li_ref[:n, :n] = m
    r = dot_full(m, d_ref[:n, n : 2 * n])
    d_ref[:n, n : 2 * n] = r
    d_ref[n : 2 * n, n : 2 * n] = d_ref[n : 2 * n, n : 2 * n] - dot_full(r, r, True)
    d_ref[n : 2 * n, :n] = dot_full(r, m, True)


def factor_second(d_ref, li_ref):
    n = LEAF
    m = li_ref[:n, :n]
    r = dot_full(m, d_ref[:n, 2 * n :])
    d_ref[n : 2 * n, 2 * n :] = d_ref[n : 2 * n, 2 * n :] - dot_full(d_ref[:n, n : 2 * n], r, True)
    for j in (2, 3):
        rj = r[:, (j - 2) * n : (j - 1) * n]
        d_ref[j * n : (j + 1) * n, j * n :] = d_ref[j * n : (j + 1) * n, j * n :] - dot_full(rj, r[:, (j - 2) * n :], True)
        d_ref[j * n : (j + 1) * n, :n] = dot_full(rj, m, True)


def gather_kernel(x_ref, ar_ref, ac_ref, lo_ref, xin, xb, xt, d, li,
                  in_sem, loc_sem, sc_s, sc_r, zb_s, zb_r, xc_s, xc_r, cd_s, cd_r,
                  lc_s, lc_r, dg_s, dg_r, li_s, li_r):
    row = lax.axis_index("row")
    col = lax.axis_index("col")
    zl, y = row // 4, row % 4
    zh, x, co = col // 8, (col // 2) % 4, col % 2

    def dev(zl=zl, y=y, zh=zh, x=x, co=co):
        return (zl * 4 + y, (zh * 4 + x) * 2 + co)

    def rc(src, dst, ss, rs, to):
        return pltpu.make_async_remote_copy(
            src_ref=src, dst_ref=dst, send_sem=ss, recv_sem=rs, device_id=to, device_id_type=MESH
        )

    def piece(p, xq, zq):
        at = pl.multiple_of((4 * (xq // 2) + zq) * NB + (xq % 2) * LEAF, LEAF)
        return ar_ref.at[p, pl.ds(at, LEAF), :]

    top = row < 2
    root = (row == 0) & (col == 0)
    self_scatter = (row == co) & (x == 0)
    here = dev()

    load = pltpu.make_async_copy(x_ref.at[pl.ds(0, 4 * NB)], xin, in_sem)

    @pl.when(top)
    def _():
        load.start()

    bar = pltpu.get_barrier_semaphore()

    def greet(to):
        pl.semaphore_signal(bar, inc=1, device_id=to, device_id_type=MESH)

    one = lambda c: jnp.where(c, 1, 0)

    @pl.when(jnp.logical_not(self_scatter))
    def _():
        greet((co, zh * 8 + row))

    for k in range(1, 4):
        greet(dev(zh=(zh + k) % 4))
        greet(dev(x=(x + k) % 4))
    greet(dev(co=1 - co))
    edges = 7 + jnp.where(top, 4 - one(col % 8 == row), 0)
    for k in range(1, 4):
        greet(dev(y=(y + k) % 4))
    for p in range(2):

        @pl.when((row != p) & (zl == 0))
        def _():
            greet((p, col))

    edges = edges + 3 + 3 * one(top)

    @pl.when(root)
    def _():
        greet((0, 1))
        greet((1, 1))

    edges = edges + one((row < 2) & (col == 1))

    @pl.when(zl == 1)
    def _():
        greet(dev(zl=0))

    edges = edges + one(zl == 0)

    @pl.when(top)
    def _():
        load.wait()
        for q in range(4):
            v = xin[pl.ds(q, NB, stride=4), :]
            xb[:, pl.ds(q * LEAF, LEAF)] = v
            xt[pl.ds(q * LEAF, LEAF), :] = v.T

    @pl.when(root)
    def _():
        d[pl.ds(0, NB), pl.ds(0, NB)] = xb[:, pl.ds(0, NB)]
        factor_first(d, li)

    pl.semaphore_wait(bar, edges)


    def scatter(i):
        q = (x + i) % 4
        at = pl.multiple_of((4 * (q // 2) + zh) * NB + (q % 2) * LEAF, LEAF)
        return rc(xt.at[pl.ds(pl.multiple_of(q * LEAF, LEAF), LEAF)], ar_ref.at[row, pl.ds(at, LEAF), :],
                  sc_s.at[i], sc_r.at[0], (col % 8, (zh * 4 + q) * 2 + row))

    def scatter_in():
        return rc(piece(co, x, zh), piece(co, x, zh), sc_s.at[0], sc_r.at[0], dev(co=1 - co))

    def scatter_self():
        return pltpu.make_async_copy(xt.at[pl.ds(0, LEAF)], piece(co, x, zh), loc_sem.at[0])

    def z_out(k):
        q = piece(co, x, zh)
        return rc(q, q, zb_s.at[k], zb_r.at[k], dev(zh=(zh + k) % 4))

    def z_in(k):
        q = piece(co, x, (zh + 4 - k) % 4)
        return rc(q, q, zb_s.at[k], zb_r.at[k], dev(co=1 - co))

    def x_out(kz, k):
        q = piece(co, x, (zh + 4 - kz) % 4)
        return rc(q, q, xc_s.at[kz, k], xc_r.at[kz, k], dev(x=(x + (1, 3)[k]) % 4))

    def x_in(kz, k):
        q = piece(co, (x + (3, 1)[k]) % 4, (zh + 4 - kz) % 4)
        return rc(q, q, xc_s.at[kz, k], xc_r.at[kz, k], dev(co=1 - co))

    def x_relay(kz, k):
        q = piece(co, (x + (3, 1)[k]) % 4, (zh + 4 - kz) % 4).at[pl.ds(k * 64, 64)]
        return rc(q, q, xc_s.at[kz, 2 + k], xc_r.at[kz, 2 + k], dev(x=(x + (1, 3)[k]) % 4))

    def x_relay_in(kz, k):
        q = piece(co, (x + 2) % 4, (zh + 4 - kz) % 4).at[pl.ds(k * 64, 64)]
        return rc(q, q, xc_s.at[kz, 2 + k], xc_r.at[kz, 2 + k], dev(co=1 - co))

    def c_out(kz, kx):
        q = piece(co, (x + 4 - kx) % 4, (zh + 4 - kz) % 4)
        return rc(q, q, cd_s.at[kz, kx], cd_r.at[kz, kx], dev(co=1 - co))

    def c_in(kz, kx):
        q = piece(1 - co, (x + 4 - kx) % 4, (zh + 4 - kz) % 4)
        return rc(q, q, cd_s.at[kz, kx], cd_r.at[kz, kx], dev(co=1 - co))

    def lc_part(p, h):
        return ac_ref.at[pl.ds(pl.multiple_of(p * NB + h * 64, 64), 64)]

    def lc_first(p, t):
        return rc(xb.at[pl.ds(t * 64, 64)], lc_part(p, t), lc_s.at[p, t], lc_r.at[p, 0], (t, col))

    def lc_out(p, k, src=None):
        q = lc_part(p, y)
        return rc(q if src is None else src, q, lc_s.at[p, 4 + k], lc_r.at[p, k], dev(y=(y + k) % 4))

    def lc_in(p, k):
        q = lc_part(p, (y + 4 - k) % 4)
        return rc(q, q, lc_s.at[p, 4 + k], lc_r.at[p, k], dev(co=1 - co))

    def lc_cross(p, src=None):
        q = lc_part(p, y)
        return rc(q if src is None else src, q, lc_s.at[p, 4], lc_r.at[p, 0], dev(zl=1))

    def column(z, what):
        def run(cp):
            cp.start() if what == "start" else cp.wait_send()

        @pl.when(zl == z)
        def _():
            for p in range(2):
                if what == "start":
                    if z == 1:
                        lc_in(p, 0).wait_recv()
                    else:

                        @pl.when(row != p)
                        def _():
                            lc_in(p, 0).wait_recv()

                for k in range(1, 4):
                    if z == 1:
                        run(lc_out(p, k))
                    else:

                        @pl.when((row != p) & ((y + k) % 4 != p))
                        def _():
                            run(lc_out(p, k))

                        @pl.when(row == p)
                        def _():
                            run(lc_out(p, k, xb.at[pl.ds(p * 64, 64)]))

    def column_cross(what):
        for p in range(2):
            for mine in (True, False):

                @pl.when((zl == 0) & ((row == p) if mine else (row != p)))
                def _():
                    cp = lc_cross(p, xb.at[pl.ds(p * 64, 64)] if mine else None)
                    cp.start() if what == "start" else cp.wait_send()

    def column_in():
        for p in range(2):

            @pl.when(row != p)
            def _():
                for k in range(1, 4):
                    lc_in(p, k).wait_recv()

    def diag_out(p):
        return rc(xb.at[:, pl.ds(0, NB)], d.at[pl.ds(p * NB, NB), pl.ds(NB, NB)], dg_s.at[0], dg_r.at[p], (0, 0))

    def diag_in(p):
        q = d.at[pl.ds(p * NB, NB), pl.ds(NB, NB)]
        return rc(q, q, dg_s.at[0], dg_r.at[p], (0, 1))

    def li_part(ref, c):
        i, j = CHUNKS[c]
        return ref.at[pl.ds(i * LEAF, LEAF), pl.ds(j * LEAF, LEAF)]

    def li_out(c, ref, k, to):
        return rc(li_part(ref, c), li_part(lo_ref, c), li_s.at[c, k], li_r.at[c], to)

    def li_in(c):
        q = li_part(lo_ref, c)
        return rc(q, q, li_s.at[c, 0], li_r.at[c], dev(co=1 - co))

    def li_edge(c, ref, k, to, what, role):
        @pl.when(role)
        def _():
            cp = li_out(c, ref, k, to)
            cp.start() if what == "start" else cp.wait_send()

    def li_high(c, ref, what):
        mine = (row == 0) & (co == c % 2)
        for k in range(3):
            li_edge(c, ref, k, dev(x=(x + k + 1) % 4), what, mine & (zh == 0) & (x == 0))
        for k in range(2):
            li_edge(c, ref, 3 + k, dev(zh=(1, 3)[k]), what, mine & (zh == 0))
        li_edge(c, ref, 5, dev(zh=2), what, mine & (zh == 3))
        for k in range(3):
            li_edge(c, ref, 6 + k, dev(y=(y + k + 1) % 4), what, mine)

    def li_low(c, ref, what):
        mine = co == c % 2
        li_edge(c, ref, 9, dev(zl=1), what, mine & (zl == 0) & (y != 0))
        li_edge(c, ref, 6, dev(y=0), what, mine & (row == 5))
        back = mine & jnp.logical_not((row == 0) & (col == 1))
        li_edge(c, ref, 10, dev(co=1 - co), what, back if c % 2 else mine)

    def li_early(chunks):
        @pl.when((row == 0) & jnp.logical_not(root))
        def _():
            for c in chunks:
                li_in(c).wait_recv()
                li_high(c, lo_ref, "start")
                li_low(c, lo_ref, "start")

    def li_late(chunks):
        @pl.when(row != 0)
        def _():
            for c in chunks:
                li_in(c).wait_recv()
                li_low(c, lo_ref, "start")

    def li_root(i):
        @pl.when(root)
        def _():
            if i == 1:
                for p in range(2):
                    diag_in(p).wait_recv()
                factor_second(d, li)
            if i:
                factor_block(i, 4, d, li)
            for c, (a, _b) in enumerate(CHUNKS):
                if a == i:
                    if c % 2:
                        li_out(c, li, 11, dev(co=1)).start()
                    else:
                        li_high(c, li, "start")
                        li_low(c, li, "start")
                    pltpu.make_async_copy(li_part(li, c), li_part(lo_ref, c), loc_sem.at[4 + c]).start()


    for p in range(2):

        @pl.when(row == p)
        def _():
            @pl.when(col == 1)
            def _():
                diag_out(p).start()

            @pl.when(col % 8 == row)
            def _():
                scatter_self().start()

            @pl.when(col % 8 != row)
            def _():
                scatter(0).start()

            for i in range(1, 4):
                scatter(i).start()
            for t in range(4):
                if t != p:
                    lc_first(p, t).start()
            pltpu.make_async_copy(xb, ac_ref.at[pl.ds(p * NB, NB)], loc_sem.at[1]).start()

    li_root(0)
    li_root(1)


    @pl.when(self_scatter)
    def _():
        scatter_self().wait()

    @pl.when(jnp.logical_not(self_scatter))
    def _():
        scatter_in().wait_recv()

    for k in (1, 3, 2):
        z_out(k).start()
    for k in range(2):
        x_out(0, k).start()
    c_out(0, 0).start()

    li_root(2)
    li_root(3)
    li_early([0])

    def onward(kz):
        for k in range(2):
            x_out(kz, k).start()
        c_out(kz, 0).start()

    def from_x(kz):
        for k in range(2):
            x_in(kz, k).wait_recv()
            x_relay(kz, k).start()
            c_out(kz, (1, 3)[k]).start()

    def from_relay(kz):
        for k in range(2):
            x_relay_in(kz, k).wait_recv()
        c_out(kz, 2).start()

    column(0, "start")
    li_early([1, 2])
    z_in(1).wait_recv()
    onward(1)
    column_cross("start")
    for kz in (3, 2):
        z_in(kz).wait_recv()
        onward(kz)
    li_early([3, 4, 5])
    from_x(0)
    li_early([6, 7, 8, 9])
    column(1, "start")
    from_x(1)
    li_late([0, 1, 2, 3, 4, 5])
    from_x(3)
    from_x(2)
    li_late([6, 7, 8, 9])
    for kz in (0, 1, 3, 2):
        from_relay(kz)
    column_in()

    for kz in range(4):
        for kx in range(4):
            c_in(kz, kx).wait_recv()
            c_out(kz, kx).wait_send()
        for k in range(2):
            x_out(kz, k).wait_send()
            x_relay(kz, k).wait_send()

    for k in range(1, 4):
        z_out(k).wait_send()

    for p in range(2):

        @pl.when(row == p)
        def _():
            @pl.when(col == 1)
            def _():
                diag_out(p).wait_send()

            for t in range(4):
                if t != p:
                    lc_first(p, t).wait_send()
            for q in range(1, 4):
                scatter(q).wait_send()

            @pl.when(col % 8 != row)
            def _():
                scatter(0).wait_send()

            pltpu.make_async_copy(xb, ac_ref.at[pl.ds(p * NB, NB)], loc_sem.at[1]).wait()

    column(0, "wait")
    column_cross("wait")
    column(1, "wait")

    for c in range(len(CHUNKS)):

        @pl.when((row == 0) & jnp.logical_not(root & (c % 2 == 1)))
        def _():
            li_high(c, lo_ref, "wait")

        li_low(c, lo_ref, "wait")

        @pl.when(root)
        def _():
            if c % 2:
                li_out(c, li, 11, dev(co=1)).wait_send()
            pltpu.make_async_copy(li_part(li, c), li_part(lo_ref, c), loc_sem.at[4 + c]).wait()


def gather(flat):
    any_spec = pl.BlockSpec(memory_space=pl.ANY)
    dma = pltpu.SemaphoreType.DMA
    return pl.pallas_call(
        gather_kernel,
        out_shape=[
            jax.ShapeDtypeStruct((2, 2048, NB), F32),
            jax.ShapeDtypeStruct((2 * NB, 2 * NB), F32),
            jax.ShapeDtypeStruct((2 * NB, 2 * NB), F32),
        ],
        in_specs=[pl.BlockSpec(memory_space=pltpu.HBM)],
        out_specs=[any_spec] * 3,
        scratch_shapes=[
            pltpu.VMEM((4 * NB, 128), F32),
            pltpu.VMEM((NB, 2 * NB), F32),
            pltpu.VMEM((2 * NB, NB), F32),
            pltpu.VMEM((2 * NB, 2 * NB), F32),
            pltpu.VMEM((2 * NB, 2 * NB), F32),
            dma, dma((14,)),
            dma((4,)), dma((1,)),
            dma((4,)), dma((4,)),
            dma((4, 4)), dma((4, 4)),
            dma((4, 4)), dma((4, 4)),
            dma((2, 11)), dma((2, 4)),
            dma((1,)), dma((2,)),
            dma((10, 12)), dma((10,)),
        ],
        compiler_params=pltpu.CompilerParams(collective_id=0, has_side_effects=True, vmem_limit_bytes=32 << 20),
        name="gather_panel",
    )(flat)


def halves(a):
    hi = a.astype(BF16)
    return hi, (a - hi.astype(F32)).astype(BF16)


def dot3(a, b, da=1, db=0):
    mm = lambda u, v: lax.dot_general(u, v, (((da,), (db,)), ((), ())), preferred_element_type=F32)
    return mm(a[0], b[0]) + (mm(a[0], b[1]) + mm(a[1], b[0]))


def update_kernel(x_ref, ar_ref, ac_ref, li_ref, o_ref, w, a, l_hi, l_lo):
    slot = pl.program_id(0)
    row = lax.axis_index("row")
    col = lax.axis_index("col")
    kk = 2 * NB

    @pl.when(slot == 0)
    def _():
        for i in range(4):
            for j in range(4):
                at = (pl.ds(i * LEAF, LEAF), pl.ds(j * LEAF, LEAF))
                if j > i:
                    l_hi[at] = jnp.zeros((LEAF, LEAF), BF16)
                    l_lo[at] = jnp.zeros((LEAF, LEAF), BF16)
                else:
                    v = li_ref[at]
                    if i == j:
                        r = lax.broadcasted_iota(jnp.int32, v.shape, 0)
                        c = lax.broadcasted_iota(jnp.int32, v.shape, 1)
                        v = jnp.where(c <= r, v, 0.0)
                    l_hi[at], l_lo[at] = halves(v)
        l = (l_hi[...], l_lo[...])
        u = dot3(l, halves(ac_ref[...]))
        hi, lo = halves(dot3(l, halves(u), 0))
        w[pl.ds(0, kk), :] = hi
        w[pl.ds(kk, kk), :] = lo
        w[pl.ds(2 * kk, kk), :] = hi

    for p in range(2):
        hi, lo = halves(ar_ref[p])
        a[:, pl.ds(p * NB, NB)] = hi
        a[:, pl.ds(kk + p * NB, NB)] = hi
        a[:, pl.ds(2 * kk + p * NB, NB)] = lo
    grow = slot * 8 + row
    keep = grow >= 2

    def trail(half):
        upd = jnp.dot(a[...], w[:, pl.ds(half * NB, NB)], preferred_element_type=F32)
        for q in range(2):
            at = (0, pl.ds(2 * half + q, NB, stride=4), slice(None))
            o_ref[at] = jnp.where(keep, x_ref[at] - upd[:, q * LEAF : (q + 1) * LEAF], 0.0)

    trail(1)

    @pl.when((col >= 2) | ((col == 1) & (grow == 0)))
    def _():
        trail(0)

    def put(p, mask):
        n = (p + 1) * NB
        at = (pl.ds(p * NB, NB), pl.ds(0, n))
        v2 = dot3((a[:, pl.ds(0, n)], a[:, pl.ds(2 * kk, n)]), (l_hi[at], l_lo[at]), 1, 1)
        for q in range(2):
            v = v2[:, q * LEAF : (q + 1) * LEAF]
            r = lax.broadcasted_iota(jnp.int32, v.shape, 0)
            c = lax.broadcasted_iota(jnp.int32, v.shape, 1) + q * LEAF
            o_ref[0, pl.ds(q, NB, stride=4), :] = jnp.where((c <= r) | jnp.logical_not(mask), v, 0.0)

    @pl.when(col == 0)
    def _():
        put(0, grow == 0)

    @pl.when((col == 1) & (grow >= 1))
    def _():
        put(1, grow == 1)


def update(flat, ar, ac, li):
    whole = pl.BlockSpec((2 * NB, 2 * NB), lambda s: (0, 0))
    slab = pl.BlockSpec((1, 4 * NB, 128), lambda s: (s, 0, 0))
    return pl.pallas_call(
        update_kernel,
        grid=(8,),
        out_shape=jax.ShapeDtypeStruct(flat.shape, F32),
        in_specs=[slab, pl.BlockSpec((2, NB, NB), lambda s: (0, s, 0)), whole, whole],
        out_specs=slab,
        scratch_shapes=[
            pltpu.VMEM((6 * NB, 2 * NB), BF16),
            pltpu.VMEM((NB, 6 * NB), BF16),
            pltpu.VMEM((2 * NB, 2 * NB), BF16),
            pltpu.VMEM((2 * NB, 2 * NB), BF16),
        ],
        compiler_params=pltpu.CompilerParams(vmem_limit_bytes=32 << 20),
        name="update_trailing",
    )(flat, ar, ac, li)


def body(matrix):
    flat = matrix.reshape(8 * 4 * NB, 128)
    ar, ac, li = gather(flat)
    return update(flat.reshape(8, 4 * NB, 128), ar, ac, li).reshape(matrix.shape)


def solution(mesh):
    spec = P(None, "row", None, None, "col", None)
    return jax.shard_map(body, mesh=mesh, in_specs=(spec,), out_specs=spec, check_vma=False)
```

time: 89.4 us -> 79.7 us (0.89)
  the two profiles are of different devices: /device:TPU:117 before, /device:TPU:101 now
where the time goes in v2:
time: 79.7 us; the launch traced here: 79.6 us
  Pallas kernels  77.4 us (97%)
  local copies, waits for them, and re-layouts  2.19 us (3%)
    pallas_call x1, Pallas kernels, gather(): pl.pallas_call(gather_kernel, out_shape=[jax.ShapeDtypeStruct((2, 2048, N...  68.1 us
    pallas_call x1, Pallas kernels, update(): pl.pallas_call(update_kernel, grid=(8,), out_shape=jax.ShapeDtypeStruct(f...  9.27 us
    unnamed x2, local copies, waits for them, and re-layouts  2.19 us

profile of v2, /device:TPU:101, one launch (start us, length us, event | category | flops | bytes accessed | tf_op | source)
XLA Modules:
  0.0 79.6 jit_solution(9009693613692417415)
XLA Ops:
  0.0 0.0 copy-start
  0.0 2.2 %copy-done = f32[8,1,256,2,1,256]{5,4,3,2,1,0:T(1,128)S(1)} copy-done((f32[8,1,256,2,1,256]{5,4,3,2,1,0:T(1,128)S(1)}, f32[8,1,256,2,1,256]{5,4,3,2,1,0:T(1,128)}, u32[]{:S(2)}) %copy-start) | copy-done | bytes 4194328
  2.2 68.1 %gather_panel.1 = (f32[2,2048,256]{2,1,0:T(8,128)S(1)}, f32[512,512]{1,0:T(8,128)S(1)}, f32[512,512]{1,0:T(8,128)S(1)}) custom-call(f32[8192,128]{1,0:T(8,128)S(1)} %bitcast.3), custom_call_target="tpu_custom_call" | custom-call | tf_op jit(solution)/shard_map/gather_panel/pallas_call | solution.py:494
  70.3 9.3 %update_trailing.1 = f32[8,1024,128]{2,1,0:T(8,128)} custom-call(f32[8,1024,128]{2,1,0:T(8,128)S(1)} %bitcast.4, f32[2,2048,256]{2,1,0:T(8,128)S(1)} %get-tuple-element.8.ar_ref, f32[512,512]{1,0:T(8,128)S(1)} %get-tuple-element.9.ac_ref, f32[512,512]{1,0:T(8,128)S(1)} %get-tuple-element.10.li_ref), custom_call_target="tpu_custom_call" | custom-call | tf_op jit(solution)/shard_map/update_trailing/pallas_call | solution.py:603
Async XLA Ops:
  0.0 2.2 %copy-start = (f32[8,1,256,2,1,256]{5,4,3,2,1,0:T(1,128)S(1)}, f32[8,1,256,2,1,256]{5,4,3,2,1,0:T(1,128)}, u32[]{:S(2)}) copy-start(f32[8,1,256,2,1,256]{5,4,3,2,1,0:T(1,128)} %param.1) | copy-start | bytes 12582916

commit v3 on v2

--- a/solution.py
+++ b/solution.py
@@ -12,6 +12,7 @@
 NB = 256
 LEAF = 128
 CHUNKS = [(i, j) for i in range(4) for j in range(i + 1)]
+STAGES = [[0, 1, 2], [3, 4], [5, 6, 7, 8], [9]]
 
 
 def leaf_inverse(block):
@@ -49,11 +50,13 @@
 def factor_block(i, nb, d_ref, li_ref):
     n = LEAF
     s = slice(i * n, (i + 1) * n)
-    m = leaf_inverse(d_ref[s, s])
-    li_ref[s, s] = m
-    if i:
+    if i == 1:
+        m = li_ref[s, s]
+    else:
+        m = leaf_inverse(d_ref[s, s])
+        li_ref[s, s] = m
+    if i + 1 < nb:
         li_ref[s, : i * n] = -dot_full(m, d_ref[s, : i * n])
-    if i + 1 < nb:
         r = dot_full(m, d_ref[s, (i + 1) * n :])
         for j in range(i + 1, nb):
             off = (j - i - 1) * n
@@ -74,6 +77,7 @@
     d_ref[:n, n : 2 * n] = r
     d_ref[n : 2 * n, n : 2 * n] = d_ref[n : 2 * n, n : 2 * n] - dot_full(r, r, True)
     d_ref[n : 2 * n, :n] = dot_full(r, m, True)
+    li_ref[n : 2 * n, n : 2 * n] = leaf_inverse(d_ref[n : 2 * n, n : 2 * n])
 
 
 def factor_second(d_ref, li_ref):
@@ -155,7 +159,11 @@
     def _():
         greet(dev(zl=0))
 
-    edges = edges + one(zl == 0)
+    @pl.when(row == 4)
+    def _():
+        greet(dev(zl=0, zh=(zh + 1) % 4))
+
+    edges = edges + one(zl == 0) + one(row == 0)
 
     @pl.when(top)
     def _():
@@ -291,6 +299,9 @@
     def li_part(ref, c):
         i, j = CHUNKS[c]
         return ref.at[pl.ds(i * LEAF, LEAF), pl.ds(j * LEAF, LEAF)]
+
+    def source_of(c):
+        return li if CHUNKS[c][0] == CHUNKS[c][1] else d
 
     def li_out(c, ref, k, to):
         return rc(li_part(ref, c), li_part(lo_ref, c), li_s.at[c, k], li_r.at[c], to)
@@ -318,7 +329,7 @@
     def li_low(c, ref, what):
         mine = co == c % 2
         li_edge(c, ref, 9, dev(zl=1), what, mine & (zl == 0) & (y != 0))
-        li_edge(c, ref, 6, dev(y=0), what, mine & (row == 5))
+        li_edge(c, ref, 9, (4, ((zh + 3) % 4 * 4 + x) * 2 + co), what, mine & (row == 0))
         back = mine & jnp.logical_not((row == 0) & (col == 1))
         li_edge(c, ref, 10, dev(co=1 - co), what, back if c % 2 else mine)
 
@@ -346,14 +357,14 @@
                 factor_second(d, li)
             if i:
                 factor_block(i, 4, d, li)
-            for c, (a, _b) in enumerate(CHUNKS):
-                if a == i:
-                    if c % 2:
-                        li_out(c, li, 11, dev(co=1)).start()
-                    else:
-                        li_high(c, li, "start")
-                        li_low(c, li, "start")
-                    pltpu.make_async_copy(li_part(li, c), li_part(lo_ref, c), loc_sem.at[4 + c]).start()
+            for c in STAGES[i]:
+                ref = source_of(c)
+                if c % 2:
+                    li_out(c, ref, 11, dev(co=1)).start()
+                else:
+                    li_high(c, ref, "start")
+                    li_low(c, ref, "start")
+                pltpu.make_async_copy(li_part(ref, c), li_part(lo_ref, c), loc_sem.at[4 + c]).start()
 
 
     for p in range(2):
@@ -399,7 +410,7 @@
 
     li_root(2)
     li_root(3)
-    li_early([0])
+    li_early(STAGES[0])
 
     def onward(kz):
         for k in range(2):
@@ -418,22 +429,22 @@
         c_out(kz, 2).start()
 
     column(0, "start")
-    li_early([1, 2])
+    li_early(STAGES[1])
     z_in(1).wait_recv()
     onward(1)
     column_cross("start")
     for kz in (3, 2):
         z_in(kz).wait_recv()
         onward(kz)
-    li_early([3, 4, 5])
+    li_early(STAGES[2])
     from_x(0)
-    li_early([6, 7, 8, 9])
+    li_early(STAGES[3])
     column(1, "start")
     from_x(1)
-    li_late([0, 1, 2, 3, 4, 5])
+    li_late(STAGES[0] + STAGES[1])
     from_x(3)
     from_x(2)
-    li_late([6, 7, 8, 9])
+    li_late(STAGES[2] + STAGES[3])
     for kz in (0, 1, 3, 2):
         from_relay(kz)
     column_in()
@@ -484,8 +495,8 @@
         @pl.when(root)
         def _():
             if c % 2:
-                li_out(c, li, 11, dev(co=1)).wait_send()
-            pltpu.make_async_copy(li_part(li, c), li_part(lo_ref, c), loc_sem.at[4 + c]).wait()
+                li_out(c, source_of(c), 11, dev(co=1)).wait_send()
+            pltpu.make_async_copy(li_part(source_of(c), c), li_part(lo_ref, c), loc_sem.at[4 + c]).wait()
 
 
 def gather(flat):
@@ -538,19 +549,20 @@
 
     @pl.when(slot == 0)
     def _():
+        zero = jnp.zeros((LEAF, LEAF), BF16)
         for i in range(4):
-            for j in range(4):
-                at = (pl.ds(i * LEAF, LEAF), pl.ds(j * LEAF, LEAF))
-                if j > i:
-                    l_hi[at] = jnp.zeros((LEAF, LEAF), BF16)
-                    l_lo[at] = jnp.zeros((LEAF, LEAF), BF16)
-                else:
-                    v = li_ref[at]
-                    if i == j:
-                        r = lax.broadcasted_iota(jnp.int32, v.shape, 0)
-                        c = lax.broadcasted_iota(jnp.int32, v.shape, 1)
-                        v = jnp.where(c <= r, v, 0.0)
-                    l_hi[at], l_lo[at] = halves(v)
+            rows = pl.ds(i * LEAF, LEAF)
+            v = li_ref[rows, rows]
+            r = lax.broadcasted_iota(jnp.int32, v.shape, 0)
+            c = lax.broadcasted_iota(jnp.int32, v.shape, 1)
+            v = jnp.where(c <= r, v, 0.0)
+            l_hi[rows, rows], l_lo[rows, rows] = halves(v)
+            if i:
+                left = pl.ds(0, i * LEAF)
+                l_hi[rows, left], l_lo[rows, left] = halves(-dot_full(v, li_ref[rows, left]))
+            for j in range(i + 1, 4):
+                l_hi[rows, pl.ds(j * LEAF, LEAF)] = zero
+                l_lo[rows, pl.ds(j * LEAF, LEAF)] = zero
         l = (l_hi[...], l_lo[...])
         u = dot3(l, halves(ac_ref[...]))
         hi, lo = halves(dot3(l, halves(u), 0))

time: 79.7 us -> 77.3 us (0.970)
  the two profiles are of different devices: /device:TPU:101 before, /device:TPU:117 now
where the time goes in v3:
time: 77.3 us; the launch traced here: 77.2 us
  Pallas kernels  75 us (97%)
  local copies, waits for them, and re-layouts  2.19 us (3%)
    pallas_call x1, Pallas kernels, gather(): pl.pallas_call(gather_kernel, out_shape=[jax.ShapeDtypeStruct((2, 2048, N...  65.4 us
    pallas_call x1, Pallas kernels, update(): pl.pallas_call(update_kernel, grid=(8,), out_shape=jax.ShapeDtypeStruct(f...  9.63 us
    unnamed x2, local copies, waits for them, and re-layouts  2.19 us

profile of v3, /device:TPU:117, one launch (start us, length us, event | category | flops | bytes accessed | tf_op | source)
XLA Modules:
  0.0 77.2 jit_solution(17843995599598825183)
XLA Ops:
  0.0 0.0 copy-start
  0.0 2.2 %copy-done = f32[8,1,256,2,1,256]{5,4,3,2,1,0:T(1,128)S(1)} copy-done((f32[8,1,256,2,1,256]{5,4,3,2,1,0:T(1,128)S(1)}, f32[8,1,256,2,1,256]{5,4,3,2,1,0:T(1,128)}, u32[]{:S(2)}) %copy-start) | copy-done | bytes 4194328
  2.2 65.4 %gather_panel.1 = (f32[2,2048,256]{2,1,0:T(8,128)S(1)}, f32[512,512]{1,0:T(8,128)S(1)}, f32[512,512]{1,0:T(8,128)S(1)}) custom-call(f32[8192,128]{1,0:T(8,128)S(1)} %bitcast.3), custom_call_target="tpu_custom_call" | custom-call | tf_op jit(solution)/shard_map/gather_panel/pallas_call | solution.py:505
  67.6 9.6 %update_trailing.1 = f32[8,1024,128]{2,1,0:T(8,128)} custom-call(f32[8,1024,128]{2,1,0:T(8,128)S(1)} %bitcast.4, f32[2,2048,256]{2,1,0:T(8,128)S(1)} %get-tuple-element.8.ar_ref, f32[512,512]{1,0:T(8,128)S(1)} %get-tuple-element.9.ac_ref, f32[512,512]{1,0:T(8,128)S(1)} %get-tuple-element.10.li_ref), custom_call_target="tpu_custom_call" | custom-call | tf_op jit(solution)/shard_map/update_trailing/pallas_call | solution.py:615
Async XLA Ops:
  0.0 2.2 %copy-start = (f32[8,1,256,2,1,256]{5,4,3,2,1,0:T(1,128)S(1)}, f32[8,1,256,2,1,256]{5,4,3,2,1,0:T(1,128)}, u32[]{:S(2)}) copy-start(f32[8,1,256,2,1,256]{5,4,3,2,1,0:T(1,128)} %param.1) | copy-start | bytes 12582916

commit v4 on v3

--- a/solution.py
+++ b/solution.py
@@ -323,11 +323,12 @@
         for k in range(2):
             li_edge(c, ref, 3 + k, dev(zh=(1, 3)[k]), what, mine & (zh == 0))
         li_edge(c, ref, 5, dev(zh=2), what, mine & (zh == 3))
-        for k in range(3):
+        for k in (0, 2):
             li_edge(c, ref, 6 + k, dev(y=(y + k + 1) % 4), what, mine)
 
     def li_low(c, ref, what):
         mine = co == c % 2
+        li_edge(c, ref, 7, dev(y=2), what, mine & (row == 3))
         li_edge(c, ref, 9, dev(zl=1), what, mine & (zl == 0) & (y != 0))
         li_edge(c, ref, 9, (4, ((zh + 3) % 4 * 4 + x) * 2 + co), what, mine & (row == 0))
         back = mine & jnp.logical_not((row == 0) & (col == 1))

time: 77.3 us -> 74.1 us (0.959)
  Pallas kernels: 75 us -> 71.8 us
    pallas_call x1, Pallas kernels: 65.4 us -> 62.2 us  [gather(): pl.pallas_call(gather_kernel, out_shape=[jax.ShapeDtypeStruct((2, 2048, N...]
where the time goes in v4:
time: 74.1 us; the launch traced here: 74 us
  Pallas kernels  71.8 us (97%)
  local copies, waits for them, and re-layouts  2.19 us (3%)
    pallas_call x1, Pallas kernels, gather(): pl.pallas_call(gather_kernel, out_shape=[jax.ShapeDtypeStruct((2, 2048, N...  62.2 us
    pallas_call x1, Pallas kernels, update(): pl.pallas_call(update_kernel, grid=(8,), out_shape=jax.ShapeDtypeStruct(f...  9.63 us
    unnamed x2, local copies, waits for them, and re-layouts  2.19 us

profile of v4, /device:TPU:117, one launch (start us, length us, event | category | flops | bytes accessed | tf_op | source)
XLA Modules:
  0.0 74.0 jit_solution(7851029229670854933)
XLA Ops:
  0.0 0.0 copy-start
  0.0 2.2 %copy-done = f32[8,1,256,2,1,256]{5,4,3,2,1,0:T(1,128)S(1)} copy-done((f32[8,1,256,2,1,256]{5,4,3,2,1,0:T(1,128)S(1)}, f32[8,1,256,2,1,256]{5,4,3,2,1,0:T(1,128)}, u32[]{:S(2)}) %copy-start) | copy-done | bytes 4194328
  2.2 62.2 %gather_panel.1 = (f32[2,2048,256]{2,1,0:T(8,128)S(1)}, f32[512,512]{1,0:T(8,128)S(1)}, f32[512,512]{1,0:T(8,128)S(1)}) custom-call(f32[8192,128]{1,0:T(8,128)S(1)} %bitcast.3), custom_call_target="tpu_custom_call" | custom-call | tf_op jit(solution)/shard_map/gather_panel/pallas_call | solution.py:506
  64.4 9.6 %update_trailing.1 = f32[8,1024,128]{2,1,0:T(8,128)} custom-call(f32[8,1024,128]{2,1,0:T(8,128)S(1)} %bitcast.4, f32[2,2048,256]{2,1,0:T(8,128)S(1)} %get-tuple-element.8.ar_ref, f32[512,512]{1,0:T(8,128)S(1)} %get-tuple-element.9.ac_ref, f32[512,512]{1,0:T(8,128)S(1)} %get-tuple-element.10.li_ref), custom_call_target="tpu_custom_call" | custom-call | tf_op jit(solution)/shard_map/update_trailing/pallas_call | solution.py:616
Async XLA Ops:
  0.0 2.2 %copy-start = (f32[8,1,256,2,1,256]{5,4,3,2,1,0:T(1,128)S(1)}, f32[8,1,256,2,1,256]{5,4,3,2,1,0:T(1,128)}, u32[]{:S(2)}) copy-start(f32[8,1,256,2,1,256]{5,4,3,2,1,0:T(1,128)} %param.1) | copy-start | bytes 12582916

commit v5 on v4

--- a/solution.py
+++ b/solution.py
@@ -565,11 +565,16 @@
                 l_hi[rows, pl.ds(j * LEAF, LEAF)] = zero
                 l_lo[rows, pl.ds(j * LEAF, LEAF)] = zero
         l = (l_hi[...], l_lo[...])
-        u = dot3(l, halves(ac_ref[...]))
-        hi, lo = halves(dot3(l, halves(u), 0))
-        w[pl.ds(0, kk), :] = hi
-        w[pl.ds(kk, kk), :] = lo
-        w[pl.ds(2 * kk, kk), :] = hi
+        ch, cl = halves(ac_ref[...])
+        uh, ul = halves(dot3((l[0][:NB, :NB], l[1][:NB, :NB]), (ch[:NB], cl[:NB])))
+        vh, vl = halves(dot3((l[0][NB:], l[1][NB:]), (ch, cl)))
+        high = dot3((l[0][:NB, :NB], l[1][:NB, :NB]), (uh, ul), 0) + dot3((l[0][NB:, :NB], l[1][NB:, :NB]), (vh, vl), 0)
+        low = dot3((l[0][NB:, NB:], l[1][NB:, NB:]), (vh, vl), 0)
+        for p, part in enumerate((high, low)):
+            hi, lo = halves(part)
+            w[pl.ds(p * NB, NB), :] = hi
+            w[pl.ds(kk + p * NB, NB), :] = lo
+            w[pl.ds(2 * kk + p * NB, NB), :] = hi
 
     for p in range(2):
         hi, lo = halves(ar_ref[p])

time: 74.1 us -> 73.6 us (level)
  no operation moved by 1% of the time
where the time goes in v5:
time: 73.6 us; the launch traced here: 73.5 us
  Pallas kernels  71.3 us (97%)
  local copies, waits for them, and re-layouts  2.19 us (3%)
    pallas_call x1, Pallas kernels, gather(): pl.pallas_call(gather_kernel, out_shape=[jax.ShapeDtypeStruct((2, 2048, N...  62.2 us
    pallas_call x1, Pallas kernels, update(): pl.pallas_call(update_kernel, grid=(8,), out_shape=jax.ShapeDtypeStruct(f...  9.15 us
    unnamed x2, local copies, waits for them, and re-layouts  2.19 us

profile of v5, /device:TPU:117, one launch (start us, length us, event | category | flops | bytes accessed | tf_op | source)
XLA Modules:
  0.0 73.5 jit_solution(933035034550500428)
XLA Ops:
  0.0 0.0 copy-start
  0.0 2.2 %copy-done = f32[8,1,256,2,1,256]{5,4,3,2,1,0:T(1,128)S(1)} copy-done((f32[8,1,256,2,1,256]{5,4,3,2,1,0:T(1,128)S(1)}, f32[8,1,256,2,1,256]{5,4,3,2,1,0:T(1,128)}, u32[]{:S(2)}) %copy-start) | copy-done | bytes 4194328
  2.2 62.2 %gather_panel.1 = (f32[2,2048,256]{2,1,0:T(8,128)S(1)}, f32[512,512]{1,0:T(8,128)S(1)}, f32[512,512]{1,0:T(8,128)S(1)}) custom-call(f32[8192,128]{1,0:T(8,128)S(1)} %bitcast.3), custom_call_target="tpu_custom_call" | custom-call | tf_op jit(solution)/shard_map/gather_panel/pallas_call | solution.py:506
  64.4 9.2 %update_trailing.1 = f32[8,1024,128]{2,1,0:T(8,128)} custom-call(f32[8,1024,128]{2,1,0:T(8,128)S(1)} %bitcast.4, f32[2,2048,256]{2,1,0:T(8,128)S(1)} %get-tuple-element.8.ar_ref, f32[512,512]{1,0:T(8,128)S(1)} %get-tuple-element.9.ac_ref, f32[512,512]{1,0:T(8,128)S(1)} %get-tuple-element.10.li_ref), custom_call_target="tpu_custom_call" | custom-call | tf_op jit(solution)/shard_map/update_trailing/pallas_call | solution.py:621
Async XLA Ops:
  0.0 2.2 %copy-start = (f32[8,1,256,2,1,256]{5,4,3,2,1,0:T(1,128)S(1)}, f32[8,1,256,2,1,256]{5,4,3,2,1,0:T(1,128)}, u32[]{:S(2)}) copy-start(f32[8,1,256,2,1,256]{5,4,3,2,1,0:T(1,128)} %param.1) | copy-start | bytes 12582916
